TPU v7x, 32 devices: a whole 2x2x4 slice. The times are simulated.
32 devices in a mesh: grp: 2 (over y), space: 4 (over z), lev: 2 (over x), rk: 2 (over core).
Axes of the slice: x: 2, y: 2, z: 4, core: 2. Of those that a mesh axis runs over, the one named last changes fastest.
Arguments:
- anomaly: bfloat16 [64, 128, 16, 256], P(('grp', 'space'), None, 'lev'), parts along dimension 0, may hold values from -5 to 5
- depth: int32 [64, 128], P(('grp', 'space')), parts along dimension 0, may hold values from 0 to 16
- cell_weight: float32 [64, 128], P(('grp', 'space')), parts along dimension 0, may hold values from 0.5 to 4
- test_matrix: bfloat16 [256, 32], P(None, 'rk'), may hold values from -6 to 6
Outputs:
- eof: float32 [64, 128, 16, 32], P(('grp', 'space'), None, 'lev', 'rk'), parts along dimension 0
- coefficients: float32 [64, 256], P(('grp', 'rk')), parts along dimension 0
There are 2 independent parts, one for each index of `grp`. A program takes and returns all parts, laid end to end along the dimension named above; an argument that names none is the same for every part. Nothing has to cross between parts.
All inputs are finite; a program needn't handle non-finite values.
Results may differ from a plain program's by a relative error of at most 0.0029.
Values may be sent and summed in bfloat16 or wider, within the bound.
A program may use at most 64 MiB of HBM per device.

v0:
```python
import jax
import jax.numpy as jnp
from jax import lax
from jax.sharding import PartitionSpec as P

HIGH = lax.Precision.HIGHEST
CONTRACT_ROWS = (((0,), (0,)), ((), ()))
CONTRACT_TIME = (((1,), (1,)), ((), ()))


def inverse_factor(gram):
    lower = jnp.linalg.cholesky(gram)
    return jax.scipy.linalg.solve_triangular(
        lower, jnp.eye(gram.shape[0], dtype=jnp.float32), lower=True
    ).T


def exact_parts(values):
    high = lax.optimization_barrier(values.astype(jnp.bfloat16))
    remainder = values - high.astype(jnp.float32)
    middle = lax.optimization_barrier(remainder.astype(jnp.bfloat16))
    lowest = (remainder - middle.astype(jnp.float32)).astype(jnp.bfloat16)
    return jnp.concatenate([high, middle, lowest], axis=1)


def project_rows(values, rows):
    width = values.shape[1]
    product = lax.dot_general(
        exact_parts(values), rows, CONTRACT_ROWS, preferred_element_type=jnp.float32
    )
    return product[:width] + product[width : 2 * width] + product[2 * width :]


def local(anomaly, depth, cell_weight, test_matrix):
    lev_dev = anomaly.shape[2]
    half = test_matrix.shape[1]
    levels = lax.axis_index("lev") * lev_dev + jnp.arange(lev_dev, dtype=jnp.int32)
    wet = (levels[None, None, :] < depth[:, :, None]).astype(jnp.float32)
    data = (
        anomaly.astype(jnp.float32) * jnp.sqrt(cell_weight)[:, :, None, None] * wet[..., None]
    ).astype(jnp.bfloat16)
    rows = data.reshape(-1, anomaly.shape[3])
    start = lax.axis_index("rk") * half
    columns = lax.all_gather(test_matrix, "rk", axis=1, tiled=True)
    local_count = jnp.sum(wet)
    sketch = jnp.dot(rows, columns, preferred_element_type=jnp.float32)
    gram0, count = lax.psum(
        (jnp.dot(sketch.T, sketch, precision=HIGH), local_count), ("space", "lev")
    )
    basis0 = jnp.dot(sketch, inverse_factor(gram0), precision=HIGH)
    timerank = lax.psum(project_rows(basis0, rows), ("space", "lev")).astype(jnp.bfloat16)
    power = lax.dot_general(rows, timerank, CONTRACT_TIME, preferred_element_type=jnp.float32)
    gram1 = lax.psum(jnp.dot(power.T, power, precision=HIGH), ("space", "lev"))
    own_cols = lax.dynamic_slice_in_dim(inverse_factor(gram1), start, half, 1)
    basis = jnp.dot(power, own_cols, precision=HIGH)
    projected = lax.psum(project_rows(basis, rows), ("space", "lev"))
    root = jnp.sqrt(count)
    eof = (basis * root).reshape(anomaly.shape[0], anomaly.shape[1], lev_dev, half)
    coefficients = projected / root
    return (eof, coefficients)


def solution(mesh):
    placed = (
        P(("grp", "space"), None, "lev", None),
        P(("grp", "space"), None),
        P(("grp", "space"), None),
        P(None, "rk"),
    )
    return jax.shard_map(
        local,
        mesh=mesh,
        in_specs=placed,
        out_specs=(P(("grp", "space"), None, "lev", "rk"), P(("grp", "rk"), None)),
        check_vma=False,
    )
```

profile of v0, /device:TPU:0, one launch (start us, length us, event | category | flops | bytes accessed | tf_op | source)
XLA Modules:
  0.0 184.8 jit_solution(14068321208825880332)
XLA Ops:
  0.6 1.5 fusion.14
  2.1 0.7 sqrt.6
  2.8 2.1 %all_gather.3 = bf16[256,32]{0,1:T(8,128)(2,1)S(1)} all-gather(bf16[256,16]{0,1:T(8,128)(2,1)} %param.10), channel_id=1, replica_groups=mesh['grp'=2,'space'=4,'lev'=2,'rk'=2] {'rk'}, dimensions={1}, use_global_device_ids=true | all-gather | bytes 24576 | tf_op jit(solution)/shard_map/all_gather | solution.py:44
  5.0 0.9 compare_convert_fusion
  5.9 4.4 %multiply_convert_fusion = bf16[8,128,8,256]{3,2,1,0:T(8,128)(2,1)S(1)} fusion(bf16[8,128,8,256]{3,2,1,0:T(8,128)(2,1)} %param.7, f32[8,128,8]{2,1,0:T(8,128)S(1)} %compare_convert_fusion, f32[8,128]{1,0:T(8,128)S(1)} %sqrt.6), kind=kLoop, calls=%fused_computation | loop fusion | flops 8388608 | bytes 8425472 | tf_op jit(solution)/shard_map/convert_element_type | solution.py:41
  10.3 0.0 copy-start
  10.3 1.9 %copy-done = bf16[8,128,8,256]{3,2,1,0:T(8,128)(2,1)} copy-done((bf16[8,128,8,256]{3,2,1,0:T(8,128)(2,1)}, bf16[8,128,8,256]{3,2,1,0:T(8,128)(2,1)S(1)}, u32[]{:S(2)}) %copy-start) | copy-done | bytes 4194328
  12.2 1.3 fusion.34
  13.5 1.0 fusion.35
  14.5 38.7 %psum.35 = f32[32,32]{0,1:T(8,128)S(1)} all-reduce(f32[32,32]{0,1:T(8,128)S(1)} %fusion.35), channel_id=1, replica_groups=mesh['grp'=2,'space'=4,'lev'=2,'rk'=2] {'space','lev'}, use_global_device_ids=true, to_apply=%region_0.0 | all-reduce | flops 1024 | bytes 8192 | tf_op jit(solution)/shard_map/psum | solution.py:47
  53.2 0.1 copy.12
  53.3 2.9 %cholesky.44 = f32[32,32]{1,0:T(8,128)S(1)} custom-call(f32[32,32]{1,0:T(8,128)S(1)} %fusion.24), custom_call_target="Cholesky" | custom-call | tf_op jit(solution)/shard_map/jit(cholesky)/cholesky | solution.py:12
  56.2 0.6 compare_reduce_fusion.1
  56.9 0.7 fusion.19
  57.5 2.4 %custom-call.6 = f32[1,32,32]{1,2,0:T(8,128)S(1)} custom-call(f32[1,32,32]{2,1,0:T(8,128)S(1)} %fusion.19), custom_call_target="InvertDiagBlocksLowerTriangular" | custom-call | tf_op jit(solution)/shard_map/jit(_solve_triangular)/triangular_solve | solution.py:13
  60.0 0.0 copy-start.1
  60.0 0.2 fusion.17
  60.2 1.0 fusion.32
  61.2 0.1 fusion.12
  61.3 0.2 subtract_convert_fusion
  61.5 0.6 copy-done.1
  62.2 0.8 fusion
  63.0 33.0 %psum.36 = bf16[32,256]{1,0:T(8,128)(2,1)S(1)} all-reduce(f32[32,256]{1,0:T(8,128)S(1)} %slice_add_fusion), channel_id=1, replica_groups=mesh['grp'=2,'space'=4,'lev'=2,'rk'=2] {'space','lev'}, use_global_device_ids=true, to_apply=%region_3.0 | all-reduce | flops 8192 | bytes 49152 | tf_op jit(solution)/shard_map/psum | solution.py:51
  96.0 3.5 %fusion.37 = f32[8192,32]{0,1:T(8,128)S(1)} fusion(bf16[8192,256]{1,0:T(8,128)(2,1)} %bitcast.34, bf16[32,256]{1,0:T(8,128)(2,1)S(1)} %psum.36), kind=kOutput, calls=%fused_computation.60 | convolution fusion | flops 134217728 | bytes 5259264 | tf_op jit(solution)/shard_map/dot_general | solution.py:52
  99.5 1.0 fusion.36
  100.5 33.0 %psum.37 = f32[32,32]{0,1:T(8,128)S(1)} all-reduce(f32[32,32]{0,1:T(8,128)S(1)} %fusion.36), channel_id=1, replica_groups=mesh['grp'=2,'space'=4,'lev'=2,'rk'=2] {'space','lev'}, use_global_device_ids=true, to_apply=%region_4.0 | all-reduce | flops 1024 | bytes 8192 | tf_op jit(solution)/shard_map/psum | solution.py:53
  133.5 0.1 copy.14
  133.6 2.9 %cholesky.55 = f32[32,32]{1,0:T(8,128)S(1)} custom-call(f32[32,32]{1,0:T(8,128)S(1)} %fusion.22), custom_call_target="Cholesky" | custom-call | tf_op jit(solution)/shard_map/jit(cholesky)/cholesky | solution.py:12
  136.6 0.6 compare_reduce_fusion
  137.2 0.7 fusion.20
  137.9 2.4 %custom-call.7 = f32[1,32,32]{1,2,0:T(8,128)S(1)} custom-call(f32[1,32,32]{2,1,0:T(8,128)S(1)} %fusion.20), custom_call_target="InvertDiagBlocksLowerTriangular" | custom-call | tf_op jit(solution)/shard_map/jit(_solve_triangular)/triangular_solve | solution.py:13
  140.3 0.0 copy-start.2
  140.3 0.2 fusion.15
  140.5 0.7 fusion.33
  141.2 0.1 fusion.13
  141.3 0.1 subtract_convert_fusion.1
  141.4 1.1 copy-done.2
  142.5 0.8 fusion.6
  143.4 34.0 %all-reduce = (f32[]{:T(128)}, f32[16,256]{1,0:T(8,128)S(1)}) all-reduce(f32[]{:T(128)} %fusion.14, f32[16,256]{1,0:T(8,128)S(1)} %slice_add_fusion.2), channel_id=1, replica_groups=mesh['grp'=2,'space'=4,'lev'=2,'rk'=2] {'space','lev'}, use_global_device_ids=true, to_apply=%region_6.9 | all-reduce | flops 4097 | bytes 32776 | tf_op jit(solution)/shard_map/psum | solution.py:47
  178.1 0.6 broadcast_divide_fusion
  178.7 2.6 %copy.15 = f32[8192,16]{1,0:T(8,128)} copy(f32[8192,16]{0,1:T(8,128)S(1)} %broadcast_multiply_fusion) | data formatting | bytes 1048576 | tf_op jit(solution)/shard_map/mul | solution.py:58
  181.3 3.5 %copy.16 = f32[8,128,8,16]{1,3,2,0:T(8,128)} copy(f32[8,128,8,16]{3,2,1,0:T(8,128)} %bitcast.37) | data formatting | bytes 1048576
  (8 shorter events, 0.1 us)
Async XLA Ops:
  10.3 1.9 %copy-start = (bf16[8,128,8,256]{3,2,1,0:T(8,128)(2,1)}, bf16[8,128,8,256]{3,2,1,0:T(8,128)(2,1)S(1)}, u32[]{:S(2)}) copy-start(bf16[8,128,8,256]{3,2,1,0:T(8,128)(2,1)S(1)} %multiply_convert_fusion) | copy-start | bytes 12582916
  60.0 2.2 %copy-start.1 = (bf16[8,128,8,256]{3,2,1,0:T(8,128)(2,1)S(1)}, bf16[8,128,8,256]{3,2,1,0:T(8,128)(2,1)}, u32[]{:S(2)}) copy-start(bf16[8,128,8,256]{3,2,1,0:T(8,128)(2,1)} %copy-done) | copy-start | bytes 12582916
  140.3 2.2 %copy-start.2 = (bf16[8,128,8,256]{3,2,1,0:T(8,128)(2,1)S(1)}, bf16[8,128,8,256]{3,2,1,0:T(8,128)(2,1)}, u32[]{:S(2)}) copy-start(bf16[8,128,8,256]{3,2,1,0:T(8,128)(2,1)} %copy-done) | copy-start | bytes 12582916
where the time goes:
time: 185 us
  blocking collectives  141 us (76%)
  other arithmetic  21.3 us (12%)
  local copies, waits for them, and re-layouts  10.6 us (6%)
  matrix products  10.5 us (6%)
    psum x2, blocking collectives, local(): lax.psum((jnp.dot(sketch.T, sketch, precision=HIGH), local_count), ('spac...  72.7 us
    psum x1, blocking collectives, local(): lax.psum(project_rows(basis0, rows), ('space', 'lev')).astype(jnp.bfloat16)  33 us
    psum x1, blocking collectives, local(): gram1 = lax.psum(jnp.dot(power.T, power, precision=HIGH), ('space', 'lev'))  33 us
    another operation x6, other arithmetic, inverse_factor(): lower = jnp.linalg.cholesky(gram)  7.19 us
    unnamed x7, local copies, waits for them, and re-layouts  7.18 us
    another operation x4, other arithmetic, inverse_factor(): jax.scipy.linalg.solve_triangular(lower, jnp.eye(gram.shape[0], dtype=jnp...  6.17 us
    convert_element_type x1, other arithmetic, local(): data = (anomaly.astype(jnp.float32) * jnp.sqrt(cell_weight)[:, :, None, N...  4.4 us

commit v1 on v0

v1 whole, which is shorter than its diff:
```python
import functools

import jax
import jax.numpy as jnp
from jax import lax
from jax.experimental import pallas as pl
from jax.experimental.pallas import tpu as pltpu
from jax.sharding import PartitionSpec as P

MESH = pl.DeviceIdType.MESH
F32 = jnp.float32
BF16 = jnp.bfloat16
OWNERS = 16
LAST = (((1,), (1,)), ((), ()))


def exact_parts(values):
    high = values.astype(BF16)
    remainder = values - high.astype(F32)
    middle = remainder.astype(BF16)
    lowest = (remainder - middle.astype(F32)).astype(BF16)
    return jnp.concatenate([high, middle, lowest], axis=0)


def sum_parts(stacked, width):
    return stacked[:width] + stacked[width : 2 * width] + stacked[2 * width :]


def dot_last(left, right):
    return lax.dot_general(left, right, LAST, preferred_element_type=F32)


def forward_eliminate(gram, sides, outs):
    rank = gram.shape[0]
    groups = rank // 8
    cols = []
    for g in range(groups):
        cols.append([jnp.broadcast_to(gram[8 * g :, c : c + 1], (rank - 8 * g, 128)) for c in range(8 * g, 8 * g + 8)])
    sides = [list(jnp.split(side, groups, axis=0)) for side in sides]
    rows = lax.broadcasted_iota(jnp.int32, (8, 128), 0)
    for k in range(rank):
        g, at = divmod(k, 8)
        column = cols[g][at]
        pivot = jnp.broadcast_to(column[at : at + 1, :], (8, 128))
        scale = lax.rsqrt(pivot)
        scale = scale * (1.5 - 0.5 * pivot * scale * scale)
        lower = []
        for i in range(g, groups):
            piece = column[8 * (i - g) : 8 * (i - g) + 8] * scale
            if i == g:
                piece = jnp.where(rows > at, piece, 0.0)
            lower.append(piece)
        for side, out in zip(sides, outs):
            width = side[0].shape[1]
            row = side[g][at : at + 1, :] * jnp.concatenate([scale[:1]] * (width // 128), axis=1)
            out[k : k + 1, :] = row
            for i in range(g, groups):
                side[i] = side[i] - jnp.concatenate([lower[i - g]] * (width // 128), axis=1) * row
        for i in range(g, groups):
            tall = lower[i - g] if i == groups - 1 else jnp.concatenate(lower[i - g :], axis=0)
            for c in range(8):
                if 8 * i + c > k:
                    cols[i][c] = cols[i][c] - tall * lower[i - g][c : c + 1, :]


def kernel(space_n, lev_n, rk_n, x_hbm, depth_ref, weight_ref, t_ref, eof_ref, coef_ref,
           x_buf, xf, data, t_all, mine, parts_a, sum_a, all_a, parts_b, sum_b, all_b,
           full, solved, solved_t, in_sem, t_sem, send_sem, recv_sem):
    n = space_n * lev_n * rk_n
    blocks, block_rows, time = x_hbm.shape
    cols = depth_ref.shape[1]
    levels = block_rows // cols
    half = t_ref.shape[0]
    rank = rk_n * half
    own_blocks = blocks // rk_n
    space, lev, rk = lax.axis_index("space"), lax.axis_index("lev"), lax.axis_index("rk")
    me = (space * lev_n + lev) * rk_n + rk

    def device(index):
        return {"space": index // (lev_n * rk_n), "lev": (index // rk_n) % lev_n, "rk": index % rk_n}

    def other(step):
        return (me + step) % n

    def each_other(body):
        if n <= 16:
            for step in range(1, n):
                body(step)
        else:
            @pl.loop(1, n)
            def _(step):
                body(step)

    def block_of(slot):
        return (rk * own_blocks + slot) % blocks

    def load(slot):
        return pltpu.make_async_copy(x_hbm.at[block_of(slot)], x_buf.at[slot], in_sem.at[slot])

    for slot in range(blocks):
        load(slot).start()

    barrier = pltpu.get_barrier_semaphore()
    each_other(lambda step: pl.semaphore_signal(barrier, inc=1, device_id=device(other(step)), device_id_type=MESH))

    t_all[rk] = t_ref[...]
    level0 = (lev * levels).astype(F32)

    def scale_slot(slot):
        block = block_of(slot)
        load(slot).wait()
        root = jnp.broadcast_to(jnp.sqrt(weight_ref[pl.ds(block, 1), :]), (128, cols)).T
        deep = jnp.broadcast_to(depth_ref[pl.ds(block, 1), :].astype(F32), (128, cols)).T
        for h in range(time // 128):
            xf[h] = x_buf[slot, :, 128 * h : 128 * h + 128].astype(F32)
        for l in range(levels):
            factor = jnp.where(level0 + l < deep, root, 0.0)
            for h in range(time // 128):
                value = xf[h, pl.ds(l, cols, stride=levels), :] * factor
                data[slot, l * cols : (l + 1) * cols, 128 * h : 128 * h + 128] = value.astype(BF16)

    def project(left, slot):
        rows = data[slot]
        parts = exact_parts(dot_last(left, rows))
        return sum_parts(jnp.dot(parts, rows, preferred_element_type=F32), rank)

    def pieces_of(full_value, extra):
        for p in range(OWNERS):
            q, h = divmod(p, 2)
            mine[p, 0:4, :] = full_value[4 * q : 4 * q + 4, 128 * h : 128 * h + 128]
            mine[p, 4:5, :] = extra

    def all_sum(value, extra, parts, total, gathered, base, between):
        pieces_of(value, extra)
        owner = None if n == OWNERS else me < OWNERS

        def when_owner(body):
            body() if owner is None else pl.when(owner)(body)

        def scatter(step):
            target = other(step)
            return pltpu.make_async_remote_copy(
                src_ref=mine.at[target % OWNERS], dst_ref=parts.at[me],
                send_sem=send_sem.at[base, target], recv_sem=recv_sem.at[base, me],
                device_id=device(target), device_id_type=MESH)

        def scattered(step):
            source = other(step)
            return pltpu.make_async_remote_copy(
                src_ref=mine.at[0], dst_ref=parts.at[source],
                send_sem=send_sem.at[base, source], recv_sem=recv_sem.at[base, source],
                device_id=device(source), device_id_type=MESH)

        def to_owner(step, body):
            body() if owner is None else pl.when(other(step) < OWNERS)(body)

        each_other(lambda step: to_owner(step, lambda: scatter(step).start()))
        between()

        def reduce():
            parts[me] = mine[me % OWNERS]
            each_other(lambda step: scattered(step).wait_recv())
            total[...] = jnp.sum(parts[...], axis=0)
            gathered[me % OWNERS] = total[...]

        when_owner(reduce)

        def spread(step):
            target = other(step)
            return pltpu.make_async_remote_copy(
                src_ref=total, dst_ref=gathered.at[me % OWNERS],
                send_sem=send_sem.at[base + 1, target], recv_sem=recv_sem.at[base + 1, me],
                device_id=device(target), device_id_type=MESH)

        def spreaded(step):
            source = other(step)
            return pltpu.make_async_remote_copy(
                src_ref=total, dst_ref=gathered.at[source % OWNERS],
                send_sem=send_sem.at[base + 1, source], recv_sem=recv_sem.at[base + 1, source],
                device_id=device(source), device_id_type=MESH)

        when_owner(lambda: each_other(lambda step: spread(step).start()))
        each_other(lambda step: to_owner(step, lambda: scatter(step).wait_send()))
        each_other(lambda step: to_owner(step, lambda: spreaded(step).wait_recv()))
        for p in range(OWNERS):
            q, h = divmod(p, 2)
            full[4 * q : 4 * q + 4, 128 * h : 128 * h + 128] = gathered[p, 0:4, :]

        def finish():
            when_owner(lambda: each_other(lambda step: spread(step).wait_send()))

        return full[...], gathered[0, 4:5, :], finish

    def scale_first(slot, carry):
        scale_slot(slot)
        return carry

    lax.fori_loop(0, own_blocks, scale_first, 0)

    pl.semaphore_wait(barrier, n - 1)
    partner = {"rk": 1 - rk}
    t_copy = pltpu.make_async_remote_copy(
        src_ref=t_ref, dst_ref=t_all.at[rk], send_sem=t_sem.at[0], recv_sem=t_sem.at[1],
        device_id=partner, device_id_type=MESH)
    t_copy.start()
    t_copy.wait()
    test = t_all[...].reshape(rank, time)

    depths = depth_ref[pl.ds(rk * own_blocks, own_blocks), :].astype(F32)
    wet = jnp.clip(depths - level0, 0.0, float(levels))
    local_count = jnp.broadcast_to(jnp.sum(wet, keepdims=True), (1, 128))

    def both(left):
        return lax.fori_loop(0, own_blocks, lambda slot, acc: acc + project(left, slot), jnp.zeros((rank, time), F32))

    first = both(test)

    def rest():
        lax.fori_loop(own_blocks, blocks, scale_first, 0)

    z, count, finish_a = all_sum(first, local_count, parts_a, sum_a, all_a, 0, rest)
    gram0 = sum_parts(dot_last(exact_parts(z), test), rank)
    forward_eliminate(gram0, [z], [solved])
    finish_a()
    timerank = solved[...].astype(BF16)

    second = both(timerank)
    w, _, finish_b = all_sum(second, local_count, parts_b, sum_b, all_b, 2, lambda: None)
    gram1 = sum_parts(dot_last(exact_parts(w), timerank), rank)
    forward_eliminate(gram1, [w, timerank.astype(F32)], [solved, solved_t])
    finish_b()
    root_count = jnp.sqrt(jnp.concatenate([count] * (time // 128), axis=1))
    own = pl.ds(pl.multiple_of(rk * half, half), half)
    coef_ref[...] = solved[own, :] / root_count
    pattern = exact_parts(solved_t[own, :] * root_count)

    def emit(slot, carry):
        e = sum_parts(dot_last(pattern, data[slot]), half)
        block = block_of(slot)
        for l in range(levels):
            eof_ref[block, l] = e[:, l * cols : (l + 1) * cols]
        return carry

    lax.fori_loop(0, blocks, emit, 0)


def local(space_n, lev_n, rk_n, anomaly, depth, cell_weight, test_matrix):
    blocks, cols, levels, time = anomaly.shape
    half = test_matrix.shape[1]
    rank = rk_n * half
    n = space_n * lev_n * rk_n
    piece = (5, 128)
    vmem = pl.BlockSpec(memory_space=pltpu.VMEM)
    eof, coefficients = pl.pallas_call(
        functools.partial(kernel, space_n, lev_n, rk_n),
        out_shape=(jax.ShapeDtypeStruct((blocks, levels, half, cols), F32), jax.ShapeDtypeStruct((half, time), F32)),
        in_specs=[pl.BlockSpec(memory_space=pl.ANY), vmem, vmem, vmem],
        out_specs=(vmem, vmem),
        scratch_shapes=[
            pltpu.VMEM((blocks, cols * levels, time), BF16),
            pltpu.VMEM((time // 128, cols * levels, 128), F32),
            pltpu.VMEM((blocks, cols * levels, time), BF16),
            pltpu.VMEM((rk_n, half, time), BF16),
            pltpu.VMEM((OWNERS, *piece), F32),
            pltpu.VMEM((n, *piece), F32), pltpu.VMEM(piece, F32), pltpu.VMEM((OWNERS, *piece), F32),
            pltpu.VMEM((n, *piece), F32), pltpu.VMEM(piece, F32), pltpu.VMEM((OWNERS, *piece), F32),
            pltpu.VMEM((rank, time), F32), pltpu.VMEM((rank, time), F32), pltpu.VMEM((rank, time), F32),
            pltpu.SemaphoreType.DMA((blocks,)),
            pltpu.SemaphoreType.DMA((2,)),
            pltpu.SemaphoreType.DMA((4, n)),
            pltpu.SemaphoreType.DMA((4, n)),
        ],
        compiler_params=pltpu.CompilerParams(
            collective_id=0, has_side_effects=True, vmem_limit_bytes=40 * 1024 * 1024),
        name="eof_power_pass",
    )(anomaly.reshape(blocks, cols * levels, time), depth, cell_weight, test_matrix.T)
    return eof.transpose(0, 3, 1, 2), coefficients


def solution(mesh):
    placed = (
        P(("grp", "space"), None, "lev", None),
        P(("grp", "space"), None),
        P(("grp", "space"), None),
        P(None, "rk"),
    )
    sizes = [mesh.shape[axis] for axis in ("space", "lev", "rk")]
    return jax.shard_map(
        functools.partial(local, *sizes),
        mesh=mesh,
        in_specs=placed,
        out_specs=(P(("grp", "space"), None, "lev", "rk"), P(("grp", "rk"), None)),
        check_vma=False,
    )
```

time: 185 us -> 39.1 us (0.21)
  blocking collectives: 141 us -> 0 us
  Pallas kernels: 0 us -> 32.6 us
  other arithmetic: 21.3 us -> 0 us
  matrix products: 10.5 us -> 0 us
  local copies, waits for them, and re-layouts: 10.6 us -> 5.65 us
    psum x4 -> x0, blocking collectives: 139 us -> none  [the longest x2 72.7 us: local(): lax.psum((jnp.dot(sketch.T, sketch, precision=HIGH), local_count), ('spac...]
    pallas_call x0 -> x1, Pallas kernels: none -> 32.6 us  [local(): pl.pallas_call(functools.partial(kernel, space_n, lev_n, rk_n), out_shape...]
    another operation x10 -> x0, other arithmetic: 13.4 us -> none  [the longest x6 7.19 us: inverse_factor(): lower = jnp.linalg.cholesky(gram)]
    dot_general x8 -> x0, matrix products: 10.1 us -> none  [the longest x1 3.5 us: local(): lax.dot_general(rows, timerank, CONTRACT_TIME, preferred_element_type=jnp...]
    convert_element_type x6 -> x0, other arithmetic: 5.75 us -> none  [the longest x1 4.4 us: local(): data = (anomaly.astype(jnp.float32) * jnp.sqrt(cell_weight)[:, :, None, N...]
    mul x1 -> x0, local copies, waits for them, and re-layouts: 2.6 us -> none  [local(): basis * root]
    all_gather x1 -> x0, blocking collectives: 2.15 us -> none  [local(): columns = lax.all_gather(test_matrix, 'rk', axis=1, tiled=True)]
    unnamed x7 -> x10, local copies, waits for them, and re-layouts: 7.18 us -> 5.65 us
where the time goes in v1:
time: 39.1 us; the launch traced here: 38.9 us
  Pallas kernels  32.6 us (83%)
  local copies, waits for them, and re-layouts  5.65 us (14%)
  between operations  0.65 us (2%)
    pallas_call x1, Pallas kernels, local(): pl.pallas_call(functools.partial(kernel, space_n, lev_n, rk_n), out_shape...  32.6 us
    unnamed x10, local copies, waits for them, and re-layouts  5.65 us

profile of v1, /device:TPU:0, one launch (start us, length us, event | category | flops | bytes accessed | tf_op | source)
XLA Modules:
  0.0 38.9 jit_solution(2639371541910389593)
XLA Ops:
  0.6 0.0 copy-start
  0.6 2.2 %copy-done = bf16[8,128,8,256]{3,2,1,0:T(8,128)(2,1)S(1)} copy-done((bf16[8,128,8,256]{3,2,1,0:T(8,128)(2,1)S(1)}, bf16[8,128,8,256]{3,2,1,0:T(8,128)(2,1)}, u32[]{:S(2)}) %copy-start) | copy-done | bytes 4194328
  2.8 0.0 copy-start.1
  2.8 0.7 %copy-done.1 = bf16[256,16]{0,1:T(8,128)(2,1)S(1)} copy-done((bf16[256,16]{0,1:T(8,128)(2,1)S(1)}, bf16[256,16]{0,1:T(8,128)(2,1)}, u32[]{:S(2)}) %copy-start.1) | copy-done | bytes 8216
  3.5 0.0 copy-start.2
  3.5 0.7 %copy-done.2 = s32[8,128]{1,0:T(8,128)S(1)} copy-done((s32[8,128]{1,0:T(8,128)S(1)}, s32[8,128]{1,0:T(8,128)}, u32[]{:S(2)}) %copy-start.2) | copy-done | bytes 4120
  4.2 0.0 copy-start.3
  4.2 0.7 %copy-done.3 = f32[8,128]{1,0:T(8,128)S(1)} copy-done((f32[8,128]{1,0:T(8,128)S(1)}, f32[8,128]{1,0:T(8,128)}, u32[]{:S(2)}) %copy-start.3) | copy-done | bytes 4120
  4.9 32.6 %eof_power_pass.1 = (f32[8,8,16,128]{3,2,1,0:T(8,128)S(1)}, f32[16,256]{1,0:T(8,128)S(1)}) custom-call(bf16[8,1024,256]{2,1,0:T(8,128)(2,1)S(1)} %bitcast.3, s32[8,128]{1,0:T(8,128)S(1)} %copy-done.2, f32[8,128]{1,0:T(8,128)S(1)} %copy-done.3, bf16[16,256]{1,0:T(8,128)(2,1)S(1)} %bitcast.5), custom_call_target="tpu_custom_call" | custom-call | tf_op jit(solution)/shard_map/eof_power_pass/pallas_call | solution.py:254
  37.5 0.8 %copy.8 = f32[8,128,8,16]{1,3,2,0:T(8,128)} copy(f32[8,128,8,16]{1,3,2,0:T(8,128)S(1)} %bitcast.4) | data formatting | bytes 1048576
  38.3 0.6 %copy.9 = f32[16,256]{1,0:T(8,128)} copy(f32[16,256]{1,0:T(8,128)S(1)} %get-tuple-element.9) | data formatting | bytes 32768
Async XLA Ops:
  0.6 2.2 %copy-start = (bf16[8,128,8,256]{3,2,1,0:T(8,128)(2,1)S(1)}, bf16[8,128,8,256]{3,2,1,0:T(8,128)(2,1)}, u32[]{:S(2)}) copy-start(bf16[8,128,8,256]{3,2,1,0:T(8,128)(2,1)} %param.4) | copy-start | bytes 12582916
  2.8 0.7 %copy-start.1 = (bf16[256,16]{0,1:T(8,128)(2,1)S(1)}, bf16[256,16]{0,1:T(8,128)(2,1)}, u32[]{:S(2)}) copy-start(bf16[256,16]{0,1:T(8,128)(2,1)} %param.7) | copy-start | bytes 24580
  3.5 0.7 %copy-start.2 = (s32[8,128]{1,0:T(8,128)S(1)}, s32[8,128]{1,0:T(8,128)}, u32[]{:S(2)}) copy-start(s32[8,128]{1,0:T(8,128)} %depth_ref.1) | copy-start | bytes 12292
  4.2 0.7 %copy-start.3 = (f32[8,128]{1,0:T(8,128)S(1)}, f32[8,128]{1,0:T(8,128)}, u32[]{:S(2)}) copy-start(f32[8,128]{1,0:T(8,128)} %weight_ref.1) | copy-start | bytes 12292

commit v2 on v1

v2 whole, which is shorter than its diff:
```python
import functools

import jax
import jax.numpy as jnp
from jax import lax
from jax.experimental import pallas as pl
from jax.experimental.pallas import tpu as pltpu
from jax.sharding import PartitionSpec as P

MESH = pl.DeviceIdType.MESH
F32 = jnp.float32
BF16 = jnp.bfloat16
OWNERS = 8
LAST = (((1,), (1,)), ((), ()))


def exact_parts(values):
    high = values.astype(BF16)
    remainder = values - high.astype(F32)
    middle = remainder.astype(BF16)
    lowest = (remainder - middle.astype(F32)).astype(BF16)
    return jnp.concatenate([high, middle, lowest], axis=0)


def sum_parts(stacked, width):
    return stacked[:width] + stacked[width : 2 * width] + stacked[2 * width :]


def dot_last(left, right):
    return lax.dot_general(left, right, LAST, preferred_element_type=F32)


def forward_eliminate(gram, sides, outs):
    rank = gram.shape[0]
    groups = rank // 8
    cols = []
    for g in range(groups):
        cols.append([jnp.broadcast_to(gram[8 * g :, c : c + 1], (rank - 8 * g, 128)) for c in range(8 * g, 8 * g + 8)])
    sides = [list(jnp.split(side, groups, axis=0)) for side in sides]
    rows = lax.broadcasted_iota(jnp.int32, (8, 128), 0)
    for k in range(rank):
        g, at = divmod(k, 8)
        column = cols[g][at]
        pivot = jnp.broadcast_to(column[at : at + 1, :], (8, 128))
        scale = lax.rsqrt(pivot)
        scale = scale * (1.5 - 0.5 * pivot * scale * scale)
        lower = []
        for i in range(g, groups):
            piece = column[8 * (i - g) : 8 * (i - g) + 8] * scale
            if i == g:
                piece = jnp.where(rows > at, piece, 0.0)
            lower.append(piece)
        for side, out in zip(sides, outs):
            width = side[0].shape[1]
            row = side[g][at : at + 1, :] * jnp.concatenate([scale[:1]] * (width // 128), axis=1)
            out[k : k + 1, :] = row
            for i in range(g, groups):
                side[i] = side[i] - jnp.concatenate([lower[i - g]] * (width // 128), axis=1) * row
        for i in range(g, groups):
            tall = lower[i - g] if i == groups - 1 else jnp.concatenate(lower[i - g :], axis=0)
            for c in range(8):
                if 8 * i + c > k:
                    cols[i][c] = cols[i][c] - tall * lower[i - g][c : c + 1, :]


def kernel(space_n, lev_n, rk_n, x_hbm, depth_hbm, weight_hbm, t_hbm, eof_ref, coef_ref,
           depth_ref, weight_ref, t_ref, x_buf, xf, data, t_all, mine, parts, all_g, g_parts,
           solved, solved_t, small_sem, in_sem, core_sem, send_sem, recv_sem):
    chips = space_n * lev_n
    blocks, block_rows, time = x_hbm.shape
    cols = depth_ref.shape[1]
    levels = block_rows // cols
    half = t_ref.shape[0]
    rank = rk_n * half
    g_half = time // rk_n
    piece = g_half // OWNERS
    space, lev, rk = lax.axis_index("space"), lax.axis_index("lev"), lax.axis_index("rk")
    me = space * lev_n + lev
    partner = {"rk": 1 - rk}

    def device(chip):
        return {"space": chip // lev_n, "lev": chip % lev_n}

    def each_other(body):
        if chips <= 16:
            for step in range(1, chips):
                body((me + step) % chips)
        else:
            @pl.loop(1, chips)
            def _(step):
                body((me + step) % chips)

    def if_owner(chip, body):
        body() if chips == OWNERS else pl.when(chip < OWNERS)(body)

    def load(slot):
        return pltpu.make_async_copy(x_hbm.at[slot], x_buf.at[slot], in_sem.at[slot])

    smalls = [
        pltpu.make_async_copy(source, target, small_sem.at[i])
        for i, (source, target) in enumerate(((t_hbm, t_ref), (weight_hbm, weight_ref), (depth_hbm, depth_ref)))
    ]
    for small in smalls:
        small.start()
    for slot in range(blocks):
        load(slot).start()

    barrier = pltpu.get_barrier_semaphore()
    pl.semaphore_signal(barrier, inc=1, device_id=partner, device_id_type=MESH)
    each_other(lambda chip: pl.semaphore_signal(barrier, inc=1, device_id=device(chip), device_id_type=MESH))

    for small in smalls:
        small.wait()
    t_all[rk] = t_ref[...]
    level0 = (lev * levels).astype(F32)

    def scale_slot(slot):
        load(slot).wait()
        root = jnp.broadcast_to(jnp.sqrt(weight_ref[pl.ds(slot, 1), :]), (128, cols)).T
        deep = jnp.broadcast_to(depth_ref[pl.ds(slot, 1), :].astype(F32), (128, cols)).T
        for h in range(time // 128):
            xf[h] = x_buf[slot, :, 128 * h : 128 * h + 128].astype(F32)
        for l in range(levels):
            factor = jnp.where(level0 + l < deep, root, 0.0)
            for h in range(time // 128):
                value = xf[h, pl.ds(l, cols, stride=levels), :] * factor
                data[slot, l * cols : (l + 1) * cols, 128 * h : 128 * h + 128] = value.astype(BF16)

    g_own = pl.ds(pl.multiple_of(rk * g_half, g_half), g_half)

    def gram_slot(slot, total):
        scale_slot(slot)
        return total + lax.dot_general(
            data[slot, :, g_own], data[slot], (((0,), (0,)), ((), ())), preferred_element_type=F32)

    gram = lax.fori_loop(0, blocks, gram_slot, jnp.zeros((g_half, time), F32))
    wet = jnp.clip(depth_ref[...].astype(F32) - level0, 0.0, float(levels))
    local_count = jnp.broadcast_to(jnp.sum(wet, keepdims=True), (1, time))
    for p in range(OWNERS):
        mine[p, 0:piece, :] = gram[piece * p : piece * (p + 1)]
        mine[p, piece : piece + 1, :] = local_count

    pl.semaphore_wait(barrier, chips)

    def scatter(target):
        return pltpu.make_async_remote_copy(
            src_ref=mine.at[target % OWNERS], dst_ref=parts.at[me],
            send_sem=send_sem.at[0, target], recv_sem=recv_sem.at[0, me],
            device_id=device(target), device_id_type=MESH)

    def scattered(source):
        return pltpu.make_async_remote_copy(
            src_ref=mine.at[0], dst_ref=parts.at[source],
            send_sem=send_sem.at[0, source], recv_sem=recv_sem.at[0, source],
            device_id=device(source), device_id_type=MESH)

    def spread(target):
        return pltpu.make_async_remote_copy(
            src_ref=all_g.at[rk, me % OWNERS], dst_ref=all_g.at[rk, me % OWNERS],
            send_sem=send_sem.at[1, target], recv_sem=recv_sem.at[1, me],
            device_id=device(target), device_id_type=MESH)

    def spreaded(source):
        return pltpu.make_async_remote_copy(
            src_ref=all_g.at[rk, source % OWNERS], dst_ref=all_g.at[rk, source % OWNERS],
            send_sem=send_sem.at[1, source], recv_sem=recv_sem.at[1, source],
            device_id=device(source), device_id_type=MESH)

    each_other(lambda chip: if_owner(chip, lambda: scatter(chip).start()))
    t_copy = pltpu.make_async_remote_copy(
        src_ref=t_ref, dst_ref=t_all.at[rk], send_sem=core_sem.at[0], recv_sem=core_sem.at[1],
        device_id=partner, device_id_type=MESH)
    t_copy.start()

    def reduce():
        parts[me] = mine[me % OWNERS]
        each_other(lambda chip: scattered(chip).wait_recv())
        all_g[rk, me % OWNERS] = jnp.sum(parts[...], axis=0)
        each_other(lambda chip: spread(chip).start())

    if_owner(me, reduce)
    t_copy.wait()
    each_other(lambda chip: if_owner(chip, lambda: scatter(chip).wait_send()))
    each_other(lambda chip: if_owner(chip, lambda: spreaded(chip).wait_recv()))
    swap = pltpu.make_async_remote_copy(
        src_ref=all_g.at[rk], dst_ref=all_g.at[rk], send_sem=core_sem.at[2], recv_sem=core_sem.at[3],
        device_id=partner, device_id_type=MESH)
    swap.start()
    if_owner(me, lambda: each_other(lambda chip: spread(chip).wait_send()))
    test = t_all[...].reshape(rank, time)
    swap.wait()

    whole = all_g[:, :, 0:piece, :].reshape(time, time)
    count = all_g[0, 0, piece : piece + 1, :]
    high = whole.astype(BF16)
    remainder = whole - high.astype(F32)
    middle = remainder.astype(BF16)
    g_parts[0] = high
    g_parts[1] = middle
    g_parts[2] = (remainder - middle.astype(F32)).astype(BF16)

    def times_g(left):
        products = [jnp.dot(left, g_parts[i], preferred_element_type=F32) for i in range(3)]
        return products[0] + (products[1] + products[2])

    z = times_g(test)
    gram0 = sum_parts(dot_last(exact_parts(z), test), rank)
    forward_eliminate(gram0, [z], [solved])
    timerank = solved[...].astype(BF16)

    w = times_g(timerank)
    gram1 = sum_parts(dot_last(exact_parts(w), timerank), rank)
    forward_eliminate(gram1, [w, timerank.astype(F32)], [solved, solved_t])
    root_count = jnp.sqrt(count)
    own = pl.ds(pl.multiple_of(rk * half, half), half)
    coef_ref[...] = solved[own, :] / root_count
    pattern = exact_parts(solved_t[own, :] * root_count)

    def emit(slot, carry):
        e = sum_parts(dot_last(pattern, data[slot]), half)
        for l in range(levels):
            eof_ref[slot, l] = e[:, l * cols : (l + 1) * cols]
        return carry

    lax.fori_loop(0, blocks, emit, 0)


def local(space_n, lev_n, rk_n, anomaly, depth, cell_weight, test_matrix):
    blocks, cols, levels, time = anomaly.shape
    half = test_matrix.shape[1]
    rank = rk_n * half
    chips = space_n * lev_n
    piece = (time // (rk_n * OWNERS) + 1, time)
    vmem = pl.BlockSpec(memory_space=pltpu.VMEM)
    eof, coefficients = pl.pallas_call(
        functools.partial(kernel, space_n, lev_n, rk_n),
        out_shape=(jax.ShapeDtypeStruct((blocks, levels, half, cols), F32), jax.ShapeDtypeStruct((half, time), F32)),
        in_specs=[pl.BlockSpec(memory_space=pltpu.HBM)] * 4,
        out_specs=(vmem, vmem),
        scratch_shapes=[
            pltpu.VMEM((blocks, cols), depth.dtype),
            pltpu.VMEM((blocks, cols), F32),
            pltpu.VMEM((half, time), BF16),
            pltpu.VMEM((blocks, cols * levels, time), BF16),
            pltpu.VMEM((time // 128, cols * levels, 128), F32),
            pltpu.VMEM((blocks, cols * levels, time), BF16),
            pltpu.VMEM((rk_n, half, time), BF16),
            pltpu.VMEM((OWNERS, *piece), F32),
            pltpu.VMEM((chips, *piece), F32),
            pltpu.VMEM((rk_n, OWNERS, *piece), F32),
            pltpu.VMEM((3, time, time), BF16),
            pltpu.VMEM((rank, time), F32),
            pltpu.VMEM((rank, time), F32),
            pltpu.SemaphoreType.DMA((3,)),
            pltpu.SemaphoreType.DMA((blocks,)),
            pltpu.SemaphoreType.DMA((4,)),
            pltpu.SemaphoreType.DMA((2, chips)),
            pltpu.SemaphoreType.DMA((2, chips)),
        ],
        compiler_params=pltpu.CompilerParams(
            collective_id=0, has_side_effects=True, vmem_limit_bytes=60 * 1024 * 1024),
        name="eof_power_pass",
    )(anomaly.reshape(blocks, cols * levels, time), depth, cell_weight, test_matrix.T)
    return eof.transpose(0, 3, 1, 2), coefficients


def solution(mesh):
    placed = (
        P(("grp", "space"), None, "lev", None),
        P(("grp", "space"), None),
        P(("grp", "space"), None),
        P(None, "rk"),
    )
    sizes = [mesh.shape[axis] for axis in ("space", "lev", "rk")]
    return jax.shard_map(
        functools.partial(local, *sizes),
        mesh=mesh,
        in_specs=placed,
        out_specs=(P(("grp", "space"), None, "lev", "rk"), P(("grp", "rk"), None)),
        check_vma=False,
    )
```

time: 39.1 us -> 30.6 us (0.78)
  Pallas kernels: 32.6 us -> 26.5 us
  local copies, waits for them, and re-layouts: 5.65 us -> 3.19 us
    pallas_call x1, Pallas kernels: 32.6 us -> 26.5 us  [local(): pl.pallas_call(functools.partial(kernel, space_n, lev_n, rk_n), out_shape...]
    unnamed x10 -> x2, local copies, waits for them, and re-layouts: 5.65 us -> 3.19 us
where the time goes in v2:
time: 30.6 us; the launch traced here: 30.3 us
  Pallas kernels  26.5 us (87%)
  local copies, waits for them, and re-layouts  3.19 us (10%)
  between operations  0.64 us (2%)
    pallas_call x1, Pallas kernels, local(): pl.pallas_call(functools.partial(kernel, space_n, lev_n, rk_n), out_shape...  26.5 us
    unnamed x2, local copies, waits for them, and re-layouts  3.19 us

profile of v2, /device:TPU:0, one launch (start us, length us, event | category | flops | bytes accessed | tf_op | source)
XLA Modules:
  0.0 30.3 jit_solution(9626086991715011186)
XLA Ops:
  0.6 26.5 %eof_power_pass.1 = (f32[8,8,16,128]{3,2,1,0:T(8,128)}, f32[16,256]{1,0:T(8,128)}) custom-call(bf16[8,1024,256]{2,1,0:T(8,128)(2,1)} %bitcast.3, s32[8,128]{1,0:T(8,128)} %depth_hbm.1, f32[8,128]{1,0:T(8,128)} %weight_hbm.1, bf16[16,256]{1,0:T(8,128)(2,1)} %bitcast.5), custom_call_target="tpu_custom_call" | custom-call | tf_op jit(solution)/shard_map/eof_power_pass/pallas_call | solution.py:235
  27.1 1.9 %copy.8 = f32[8,128,8,16]{1,3,2,0:T(8,128)} copy(f32[8,128,8,16]{1,3,2,0:T(8,128)} %bitcast.4) | data formatting | bytes 1048576
  29.0 1.3 %copy.9 = f32[16,256]{1,0:T(8,128)} copy(f32[16,256]{1,0:T(8,128)} %get-tuple-element.9) | data formatting | bytes 32768

commit v3 on v2

--- a/solution.py
+++ b/solution.py
@@ -64,7 +64,7 @@
 
 
 def kernel(space_n, lev_n, rk_n, x_hbm, depth_hbm, weight_hbm, t_hbm, eof_ref, coef_ref,
-           depth_ref, weight_ref, t_ref, x_buf, xf, data, t_all, mine, parts, all_g, g_parts,
+           depth_ref, weight_ref, t_ref, x_buf, xf, data, t_all, g_local, g_peer, mine, parts, all_g, g_parts,
            solved, solved_t, small_sem, in_sem, core_sem, send_sem, recv_sem):
     chips = space_n * lev_n
     blocks, block_rows, time = x_hbm.shape
@@ -93,8 +93,13 @@
     def if_owner(chip, body):
         body() if chips == OWNERS else pl.when(chip < OWNERS)(body)
 
+    own_blocks = blocks // rk_n
+
+    def block_of(slot):
+        return (rk * own_blocks + slot) % blocks
+
     def load(slot):
-        return pltpu.make_async_copy(x_hbm.at[slot], x_buf.at[slot], in_sem.at[slot])
+        return pltpu.make_async_copy(x_hbm.at[block_of(slot)], x_buf.at[slot], in_sem.at[slot])
 
     smalls = [
         pltpu.make_async_copy(source, target, small_sem.at[i])
@@ -115,9 +120,10 @@
     level0 = (lev * levels).astype(F32)
 
     def scale_slot(slot):
+        block = block_of(slot)
         load(slot).wait()
-        root = jnp.broadcast_to(jnp.sqrt(weight_ref[pl.ds(slot, 1), :]), (128, cols)).T
-        deep = jnp.broadcast_to(depth_ref[pl.ds(slot, 1), :].astype(F32), (128, cols)).T
+        root = jnp.broadcast_to(jnp.sqrt(weight_ref[pl.ds(block, 1), :]), (128, cols)).T
+        deep = jnp.broadcast_to(depth_ref[pl.ds(block, 1), :].astype(F32), (128, cols)).T
         for h in range(time // 128):
             xf[h] = x_buf[slot, :, 128 * h : 128 * h + 128].astype(F32)
         for l in range(levels):
@@ -126,21 +132,31 @@
                 value = xf[h, pl.ds(l, cols, stride=levels), :] * factor
                 data[slot, l * cols : (l + 1) * cols, 128 * h : 128 * h + 128] = value.astype(BF16)
 
-    g_own = pl.ds(pl.multiple_of(rk * g_half, g_half), g_half)
-
     def gram_slot(slot, total):
         scale_slot(slot)
         return total + lax.dot_general(
-            data[slot, :, g_own], data[slot], (((0,), (0,)), ((), ())), preferred_element_type=F32)
-
-    gram = lax.fori_loop(0, blocks, gram_slot, jnp.zeros((g_half, time), F32))
+            data[slot], data[slot], (((0,), (0,)), ((), ())), preferred_element_type=F32)
+
+    gram = lax.fori_loop(0, own_blocks, gram_slot, jnp.zeros((time, time), F32))
+    for r in range(rk_n):
+        g_local[r] = gram[g_half * r : g_half * (r + 1)]
     wet = jnp.clip(depth_ref[...].astype(F32) - level0, 0.0, float(levels))
     local_count = jnp.broadcast_to(jnp.sum(wet, keepdims=True), (1, time))
+
+    pl.semaphore_wait(barrier, chips)
+    halves = pltpu.make_async_remote_copy(
+        src_ref=g_local.at[1 - rk], dst_ref=g_peer, send_sem=core_sem.at[4], recv_sem=core_sem.at[5],
+        device_id=partner, device_id_type=MESH)
+    halves.start()
+    t_copy = pltpu.make_async_remote_copy(
+        src_ref=t_ref, dst_ref=t_all.at[rk], send_sem=core_sem.at[0], recv_sem=core_sem.at[1],
+        device_id=partner, device_id_type=MESH)
+    t_copy.start()
+    halves.wait()
     for p in range(OWNERS):
-        mine[p, 0:piece, :] = gram[piece * p : piece * (p + 1)]
+        rows = slice(piece * p, piece * (p + 1))
+        mine[p, 0:piece, :] = g_local[rk, rows, :] + g_peer[rows, :]
         mine[p, piece : piece + 1, :] = local_count
-
-    pl.semaphore_wait(barrier, chips)
 
     def scatter(target):
         return pltpu.make_async_remote_copy(
@@ -167,10 +183,11 @@
             device_id=device(source), device_id_type=MESH)
 
     each_other(lambda chip: if_owner(chip, lambda: scatter(chip).start()))
-    t_copy = pltpu.make_async_remote_copy(
-        src_ref=t_ref, dst_ref=t_all.at[rk], send_sem=core_sem.at[0], recv_sem=core_sem.at[1],
-        device_id=partner, device_id_type=MESH)
-    t_copy.start()
+    def scale_rest(slot, carry):
+        scale_slot(slot)
+        return carry
+
+    lax.fori_loop(own_blocks, blocks, scale_rest, 0)
 
     def reduce():
         parts[me] = mine[me % OWNERS]
@@ -218,8 +235,9 @@
 
     def emit(slot, carry):
         e = sum_parts(dot_last(pattern, data[slot]), half)
+        block = block_of(slot)
         for l in range(levels):
-            eof_ref[slot, l] = e[:, l * cols : (l + 1) * cols]
+            eof_ref[block, l] = e[:, l * cols : (l + 1) * cols]
         return carry
 
     lax.fori_loop(0, blocks, emit, 0)
@@ -234,7 +252,7 @@
     vmem = pl.BlockSpec(memory_space=pltpu.VMEM)
     eof, coefficients = pl.pallas_call(
         functools.partial(kernel, space_n, lev_n, rk_n),
-        out_shape=(jax.ShapeDtypeStruct((blocks, levels, half, cols), F32), jax.ShapeDtypeStruct((half, time), F32)),
+        out_shape=(pltpu.VMEM((blocks, levels, half, cols), F32), pltpu.VMEM((half, time), F32)),
         in_specs=[pl.BlockSpec(memory_space=pltpu.HBM)] * 4,
         out_specs=(vmem, vmem),
         scratch_shapes=[
@@ -245,6 +263,8 @@
             pltpu.VMEM((time // 128, cols * levels, 128), F32),
             pltpu.VMEM((blocks, cols * levels, time), BF16),
             pltpu.VMEM((rk_n, half, time), BF16),
+            pltpu.VMEM((rk_n, time // rk_n, time), F32),
+            pltpu.VMEM((time // rk_n, time), F32),
             pltpu.VMEM((OWNERS, *piece), F32),
             pltpu.VMEM((chips, *piece), F32),
             pltpu.VMEM((rk_n, OWNERS, *piece), F32),
@@ -253,7 +273,7 @@
             pltpu.VMEM((rank, time), F32),
             pltpu.SemaphoreType.DMA((3,)),
             pltpu.SemaphoreType.DMA((blocks,)),
-            pltpu.SemaphoreType.DMA((4,)),
+            pltpu.SemaphoreType.DMA((6,)),
             pltpu.SemaphoreType.DMA((2, chips)),
             pltpu.SemaphoreType.DMA((2, chips)),
         ],

time: 30.6 us -> 28.3 us (0.925)
  local copies, waits for them, and re-layouts: 3.19 us -> 1.4 us
  Pallas kernels: 26.5 us -> 26.1 us
    unnamed x2, local copies, waits for them, and re-layouts: 3.19 us -> 1.4 us
    pallas_call x1, Pallas kernels: 26.5 us -> 26.1 us  [local(): pl.pallas_call(functools.partial(kernel, space_n, lev_n, rk_n), out_shape...]
where the time goes in v3:
time: 28.3 us; the launch traced here: 28.2 us
  Pallas kernels  26.1 us (92%)
  local copies, waits for them, and re-layouts  1.4 us (5%)
  between operations  0.64 us (2%)
    pallas_call x1, Pallas kernels, local(): pl.pallas_call(functools.partial(kernel, space_n, lev_n, rk_n), out_shape...  26.1 us
    unnamed x2, local copies, waits for them, and re-layouts  1.4 us

profile of v3, /device:TPU:0, one launch (start us, length us, event | category | flops | bytes accessed | tf_op | source)
XLA Modules:
  0.0 28.2 jit_solution(13064526110987347205)
XLA Ops:
  0.6 26.1 %eof_power_pass.1 = (f32[8,8,16,128]{3,2,1,0:T(8,128)S(1)}, f32[16,256]{1,0:T(8,128)S(1)}) custom-call(bf16[8,1024,256]{2,1,0:T(8,128)(2,1)} %bitcast.4, s32[8,128]{1,0:T(8,128)} %depth_hbm.1, f32[8,128]{1,0:T(8,128)} %weight_hbm.1, bf16[16,256]{1,0:T(8,128)(2,1)} %bitcast.5), custom_call_target="tpu_custom_call" | custom-call | tf_op jit(solution)/shard_map/eof_power_pass/pallas_call | solution.py:253
  26.8 0.8 %copy.8 = f32[8,128,8,16]{1,3,2,0:T(8,128)} copy(f32[8,128,8,16]{1,3,2,0:T(8,128)S(1)} %bitcast.3) | data formatting | bytes 1048576
  27.5 0.6 %copy.9 = f32[16,256]{1,0:T(8,128)} copy(f32[16,256]{1,0:T(8,128)S(1)} %get-tuple-element.7) | data formatting | bytes 32768

commit v4 on v3

--- a/solution.py
+++ b/solution.py
@@ -105,14 +105,18 @@
         pltpu.make_async_copy(source, target, small_sem.at[i])
         for i, (source, target) in enumerate(((t_hbm, t_ref), (weight_hbm, weight_ref), (depth_hbm, depth_ref)))
     ]
+    load(0).start()
     for small in smalls:
         small.start()
-    for slot in range(blocks):
+    for slot in range(1, own_blocks):
         load(slot).start()
 
     barrier = pltpu.get_barrier_semaphore()
     pl.semaphore_signal(barrier, inc=1, device_id=partner, device_id_type=MESH)
     each_other(lambda chip: pl.semaphore_signal(barrier, inc=1, device_id=device(chip), device_id_type=MESH))
+
+    for slot in range(own_blocks, blocks):
+        load(slot).start()
 
     for small in smalls:
         small.wait()
@@ -125,19 +129,17 @@
         root = jnp.broadcast_to(jnp.sqrt(weight_ref[pl.ds(block, 1), :]), (128, cols)).T
         deep = jnp.broadcast_to(depth_ref[pl.ds(block, 1), :].astype(F32), (128, cols)).T
         for h in range(time // 128):
-            xf[h] = x_buf[slot, :, 128 * h : 128 * h + 128].astype(F32)
+            xf[slot % 2, h] = x_buf[slot, :, 128 * h : 128 * h + 128].astype(F32)
         for l in range(levels):
             factor = jnp.where(level0 + l < deep, root, 0.0)
             for h in range(time // 128):
-                value = xf[h, pl.ds(l, cols, stride=levels), :] * factor
+                value = xf[slot % 2, h, pl.ds(l, cols, stride=levels), :] * factor
                 data[slot, l * cols : (l + 1) * cols, 128 * h : 128 * h + 128] = value.astype(BF16)
 
-    def gram_slot(slot, total):
+    for slot in range(own_blocks):
         scale_slot(slot)
-        return total + lax.dot_general(
-            data[slot], data[slot], (((0,), (0,)), ((), ())), preferred_element_type=F32)
-
-    gram = lax.fori_loop(0, own_blocks, gram_slot, jnp.zeros((time, time), F32))
+    rows_own = data[0:own_blocks].reshape(own_blocks * block_rows, time)
+    gram = lax.dot_general(rows_own, rows_own, (((0,), (0,)), ((), ())), preferred_element_type=F32)
     for r in range(rk_n):
         g_local[r] = gram[g_half * r : g_half * (r + 1)]
     wet = jnp.clip(depth_ref[...].astype(F32) - level0, 0.0, float(levels))
@@ -240,7 +242,7 @@
             eof_ref[block, l] = e[:, l * cols : (l + 1) * cols]
         return carry
 
-    lax.fori_loop(0, blocks, emit, 0)
+    lax.fori_loop(0, blocks, emit, 0, unroll=True)
 
 
 def local(space_n, lev_n, rk_n, anomaly, depth, cell_weight, test_matrix):
@@ -260,7 +262,7 @@
             pltpu.VMEM((blocks, cols), F32),
             pltpu.VMEM((half, time), BF16),
             pltpu.VMEM((blocks, cols * levels, time), BF16),
-            pltpu.VMEM((time // 128, cols * levels, 128), F32),
+            pltpu.VMEM((2, time // 128, cols * levels, 128), F32),
             pltpu.VMEM((blocks, cols * levels, time), BF16),
             pltpu.VMEM((rk_n, half, time), BF16),
             pltpu.VMEM((rk_n, time // rk_n, time), F32),

time: 28.3 us -> 26.3 us (0.929)
  Pallas kernels: 26.1 us -> 24 us
    pallas_call x1, Pallas kernels: 26.1 us -> 24 us  [local(): pl.pallas_call(functools.partial(kernel, space_n, lev_n, rk_n), out_shape...]
where the time goes in v4:
time: 26.3 us; the launch traced here: 26.1 us
  Pallas kernels  24 us (91%)
  local copies, waits for them, and re-layouts  1.4 us (5%)
  between operations  0.64 us (2%)
    pallas_call x1, Pallas kernels, local(): pl.pallas_call(functools.partial(kernel, space_n, lev_n, rk_n), out_shape...  24 us
    unnamed x2, local copies, waits for them, and re-layouts  1.4 us

profile of v4, /device:TPU:0, one launch (start us, length us, event | category | flops | bytes accessed | tf_op | source)
XLA Modules:
  0.0 26.1 jit_solution(9002133357568918740)
XLA Ops:
  0.6 24.0 %eof_power_pass.1 = (f32[8,8,16,128]{3,2,1,0:T(8,128)S(1)}, f32[16,256]{1,0:T(8,128)S(1)}) custom-call(bf16[8,1024,256]{2,1,0:T(8,128)(2,1)} %bitcast.4, s32[8,128]{1,0:T(8,128)} %depth_hbm.1, f32[8,128]{1,0:T(8,128)} %weight_hbm.1, bf16[16,256]{1,0:T(8,128)(2,1)} %bitcast.5), custom_call_target="tpu_custom_call" | custom-call | tf_op jit(solution)/shard_map/eof_power_pass/pallas_call | solution.py:255
  24.7 0.8 %copy.8 = f32[8,128,8,16]{1,3,2,0:T(8,128)} copy(f32[8,128,8,16]{1,3,2,0:T(8,128)S(1)} %bitcast.3) | data formatting | bytes 1048576
  25.5 0.6 %copy.9 = f32[16,256]{1,0:T(8,128)} copy(f32[16,256]{1,0:T(8,128)S(1)} %get-tuple-element.7) | data formatting | bytes 32768

commit v5 on v4

--- a/solution.py
+++ b/solution.py
@@ -64,7 +64,7 @@
 
 
 def kernel(space_n, lev_n, rk_n, x_hbm, depth_hbm, weight_hbm, t_hbm, eof_ref, coef_ref,
-           depth_ref, weight_ref, t_ref, x_buf, xf, data, t_all, g_local, g_peer, mine, parts, all_g, g_parts,
+           depth_ref, weight_ref, t_ref, x_buf, xf, data, t_all, g_local, g_peer, mine, parts, all_g, whole_g, g_parts,
            solved, solved_t, small_sem, in_sem, core_sem, send_sem, recv_sem):
     chips = space_n * lev_n
     blocks, block_rows, time = x_hbm.shape
@@ -73,7 +73,9 @@
     half = t_ref.shape[0]
     rank = rk_n * half
     g_half = time // rk_n
-    piece = g_half // OWNERS
+    g_part = g_half // rk_n
+    piece, strip = g_half // OWNERS, g_part // OWNERS
+    tall = piece + strip
     space, lev, rk = lax.axis_index("space"), lax.axis_index("lev"), lax.axis_index("rk")
     me = space * lev_n + lev
     partner = {"rk": 1 - rk}
@@ -141,9 +143,12 @@
     rows_own = data[0:own_blocks].reshape(own_blocks * block_rows, time)
     gram = lax.dot_general(rows_own, rows_own, (((0,), (0,)), ((), ())), preferred_element_type=F32)
     for r in range(rk_n):
-        g_local[r] = gram[g_half * r : g_half * (r + 1)]
+        for p in range(OWNERS):
+            top, side = g_half * r + piece * p, g_part * r + strip * p
+            g_local[r, p, 0:piece, :] = gram[top : top + piece, g_half * r : g_half * (r + 1)]
+            g_local[r, p, piece:tall, :] = gram[side : side + strip, g_half:]
     wet = jnp.clip(depth_ref[...].astype(F32) - level0, 0.0, float(levels))
-    local_count = jnp.broadcast_to(jnp.sum(wet, keepdims=True), (1, time))
+    local_count = jnp.broadcast_to(jnp.sum(wet, keepdims=True), (1, g_half))
 
     pl.semaphore_wait(barrier, chips)
     halves = pltpu.make_async_remote_copy(
@@ -156,9 +161,8 @@
     t_copy.start()
     halves.wait()
     for p in range(OWNERS):
-        rows = slice(piece * p, piece * (p + 1))
-        mine[p, 0:piece, :] = g_local[rk, rows, :] + g_peer[rows, :]
-        mine[p, piece : piece + 1, :] = local_count
+        mine[p, 0:tall, :] = g_local[rk, p] + g_peer[p]
+        mine[p, tall : tall + 1, :] = local_count
 
     def scatter(target):
         return pltpu.make_async_remote_copy(
@@ -209,8 +213,14 @@
     test = t_all[...].reshape(rank, time)
     swap.wait()
 
-    whole = all_g[:, :, 0:piece, :].reshape(time, time)
-    count = all_g[0, 0, piece : piece + 1, :]
+    for r in range(rk_n):
+        for p in range(OWNERS):
+            top, side = g_half * r + piece * p, g_part * r + strip * p
+            whole_g[top : top + piece, g_half * r : g_half * (r + 1)] = all_g[r, p, 0:piece, :]
+            whole_g[side : side + strip, g_half:] = all_g[r, p, piece:tall, :]
+    whole_g[g_half:, 0:g_half] = whole_g[0:g_half, g_half:].T
+    whole = whole_g[...]
+    count = jnp.concatenate([all_g[0, 0, tall : tall + 1, :]] * rk_n, axis=1)
     high = whole.astype(BF16)
     remainder = whole - high.astype(F32)
     middle = remainder.astype(BF16)
@@ -250,7 +260,9 @@
     half = test_matrix.shape[1]
     rank = rk_n * half
     chips = space_n * lev_n
-    piece = (time // (rk_n * OWNERS) + 1, time)
+    g_half = time // rk_n
+    tall = g_half // OWNERS + g_half // (rk_n * OWNERS)
+    piece = (tall + 1, g_half)
     vmem = pl.BlockSpec(memory_space=pltpu.VMEM)
     eof, coefficients = pl.pallas_call(
         functools.partial(kernel, space_n, lev_n, rk_n),
@@ -265,11 +277,12 @@
             pltpu.VMEM((2, time // 128, cols * levels, 128), F32),
             pltpu.VMEM((blocks, cols * levels, time), BF16),
             pltpu.VMEM((rk_n, half, time), BF16),
-            pltpu.VMEM((rk_n, time // rk_n, time), F32),
-            pltpu.VMEM((time // rk_n, time), F32),
+            pltpu.VMEM((rk_n, OWNERS, tall, g_half), F32),
+            pltpu.VMEM((OWNERS, tall, g_half), F32),
             pltpu.VMEM((OWNERS, *piece), F32),
             pltpu.VMEM((chips, *piece), F32),
             pltpu.VMEM((rk_n, OWNERS, *piece), F32),
+            pltpu.VMEM((time, time), F32),
             pltpu.VMEM((3, time, time), BF16),
             pltpu.VMEM((rank, time), F32),
             pltpu.VMEM((rank, time), F32),

time: 26.3 us -> 23.7 us (0.901)
  Pallas kernels: 24 us -> 21.4 us
    pallas_call x1, Pallas kernels: 24 us -> 21.4 us  [local(): pl.pallas_call(functools.partial(kernel, space_n, lev_n, rk_n), out_shape...]
where the time goes in v5:
time: 23.7 us; the launch traced here: 23.5 us
  Pallas kernels  21.4 us (90%)
  local copies, waits for them, and re-layouts  1.4 us (6%)
  between operations  0.64 us (3%)
    pallas_call x1, Pallas kernels, local(): pl.pallas_call(functools.partial(kernel, space_n, lev_n, rk_n), out_shape...  21.4 us
    unnamed x2, local copies, waits for them, and re-layouts  1.4 us

profile of v5, /device:TPU:0, one launch (start us, length us, event | category | flops | bytes accessed | tf_op | source)
XLA Modules:
  0.0 23.5 jit_solution(13512783903414452756)
XLA Ops:
  0.6 21.4 %eof_power_pass.1 = (f32[8,8,16,128]{3,2,1,0:T(8,128)S(1)}, f32[16,256]{1,0:T(8,128)S(1)}) custom-call(bf16[8,1024,256]{2,1,0:T(8,128)(2,1)} %bitcast.4, s32[8,128]{1,0:T(8,128)} %depth_hbm.1, f32[8,128]{1,0:T(8,128)} %weight_hbm.1, bf16[16,256]{1,0:T(8,128)(2,1)} %bitcast.5), custom_call_target="tpu_custom_call" | custom-call | tf_op jit(solution)/shard_map/eof_power_pass/pallas_call | solution.py:267
  22.1 0.8 %copy.8 = f32[8,128,8,16]{1,3,2,0:T(8,128)} copy(f32[8,128,8,16]{1,3,2,0:T(8,128)S(1)} %bitcast.3) | data formatting | bytes 1048576
  22.9 0.6 %copy.9 = f32[16,256]{1,0:T(8,128)} copy(f32[16,256]{1,0:T(8,128)S(1)} %get-tuple-element.7) | data formatting | bytes 32768
